TPU v7x, 512 devices: a whole 4x8x8 slice. The times are simulated.
512 devices in a mesh: pp: 8 (over x, y_lo), cp: 64 (over y_hi, z, core).
Axes of the slice: x: 4, y: 8 (y_hi: 4, y_lo: 2; y = y_hi * 2 + y_lo), z: 8, core: 2. Of those that a mesh axis runs over, the one named last changes fastest.
Arguments:
- queries: bfloat16 [8, 2, 32, 4096, 128], P('pp', None, None, 'cp'), may hold values from -5 to 5
- keys_values: bfloat16 [8, 2, 2, 4, 4096, 128], P('pp', None, None, None, 'cp'), may hold values from -5 to 5
- old_block: int32 [128], replicated, may hold values from 0 to 127, as said below
- new_block: int32 [128], replicated, may hold values from 0 to 127, as said below
Outputs:
- section_input: bfloat16 [8, 2, 32, 4096, 128], P('pp', None, None, 'cp')
Inputs may be any that keep to these rules, and one draw needn't show every extreme that they name: `old_block`: A permutation of the sequence blocks; row-blocks 4 e to 4 e + 3 hold sequence blocks 2 a, 2 a + 1, 2 b, 2 b + 1 with a + b = 63. `new_block`: A permutation of the sequence blocks; row-blocks 2 d and 2 d + 1 hold sequence blocks c and 127 - c.
All inputs are finite; a program needn't handle non-finite values.
Results may differ from a plain program's by a relative error of at most 0.0098.
Values may be sent and summed in bfloat16 or wider, within the bound.
A program may use at most 64 MiB of HBM per device.

v0:
```python
import math
import jax
import jax.numpy as jnp
from jax import lax
from jax.sharding import PartitionSpec as P


def from_behind(value, axis, steps):
    count = lax.axis_size(axis)
    pairs = [(source, (source + steps) % count) for source in range(count)]
    return lax.ppermute(value, axis, pairs)


def regroup(tensor, block_order):
    dims_shape = tensor.shape
    count_blocks = block_order.shape[0]
    blocked = tensor.reshape(
        dims_shape[:-2] + (count_blocks, dims_shape[-2] // count_blocks, dims_shape[-1])
    )
    picked = jnp.take(blocked, block_order, axis=blocked.ndim - 3)
    return picked.reshape(dims_shape)


def rotate(tensor):
    half_dim = tensor.shape[-1] // 2
    spacing = jnp.arange(half_dim, dtype=jnp.float32) * (2.0 / tensor.shape[-1])
    inverse = jnp.exp(-spacing * jnp.log(jnp.float32(1000000.0)))
    angles = jnp.arange(tensor.shape[-2], dtype=jnp.float32)[:, None] * inverse[None, :]
    cosine = jnp.cos(angles)
    sine_part = jnp.sin(angles)
    widened = tensor.astype(jnp.float32)
    first_half = widened[..., :half_dim]
    second_half = widened[..., half_dim:]
    turned = jnp.concatenate(
        [
            first_half * cosine - second_half * sine_part,
            second_half * cosine + first_half * sine_part,
        ],
        axis=-1,
    )
    return turned.astype(jnp.bfloat16)


def causal_attend(queries, key_rows, value_rows):
    heads_here, length, head_width = queries.shape
    block_rows = min(512, length)
    block_count = length // block_rows
    score_scale = 1.0 / math.sqrt(head_width)
    offsets = jnp.arange(block_rows, dtype=jnp.int32)

    def query_step(query_index, finished):
        first_row = query_index * block_rows
        query_part = lax.dynamic_slice_in_dim(queries, first_row, block_rows, 1)
        query_pos = first_row + offsets

        def key_step(key_index, state_in):
            running, weight_sum, summed = state_in
            key_first = key_index * block_rows
            key_part = lax.dynamic_slice_in_dim(key_rows, key_first, block_rows, 0)
            value_part = lax.dynamic_slice_in_dim(value_rows, key_first, block_rows, 0)
            scores = (
                jnp.einsum("hqd,kd->hqk", query_part, key_part, preferred_element_type=jnp.float32)
                * score_scale
            )
            allowed = (key_first + offsets)[None, :] <= query_pos[:, None]
            scores = jnp.where(allowed[None], scores, -1e30)
            highest = jnp.maximum(running, jnp.max(scores, axis=-1))
            weights = jnp.exp(scores - highest[..., None])
            factor = jnp.exp(running - highest)
            weight_sum = weight_sum * factor + jnp.sum(weights, axis=-1)
            summed = summed * factor[..., None] + jnp.einsum(
                "hqk,kd->hqd",
                weights.astype(jnp.bfloat16),
                value_part,
                preferred_element_type=jnp.float32,
            )
            return (highest, weight_sum, summed)

        initial = (
            jnp.full((heads_here, block_rows), -1e30, jnp.float32),
            jnp.zeros((heads_here, block_rows), jnp.float32),
            jnp.zeros((heads_here, block_rows, head_width), jnp.float32),
        )
        running, weight_sum, summed = lax.fori_loop(0, query_index + 1, key_step, initial)
        output_block = (summed / weight_sum[..., None]).astype(jnp.bfloat16)
        return lax.dynamic_update_slice_in_dim(finished, output_block, first_row, 1)

    return lax.fori_loop(0, block_count, query_step, jnp.zeros(queries.shape, jnp.bfloat16))


def per_device(queries, keys_values, old_block, new_block):
    cp_devices = lax.axis_size("cp")
    sequences = queries.shape[1]
    query_heads = queries.shape[2]
    local_rows = queries.shape[3]
    head_width = queries.shape[4]
    kv_heads = keys_values.shape[3]
    all_items = sequences * query_heads
    items_here = all_items // cp_devices
    sharers = query_heads // kv_heads // items_here
    length = local_rows * cp_devices
    block_count = old_block.shape[0]
    sent_queries = queries.reshape(all_items, local_rows, head_width)
    heard_queries = lax.all_to_all(sent_queries, "cp", split_axis=0, concat_axis=1, tiled=True)
    pairs_local = keys_values.reshape(2, sequences, kv_heads, local_rows, head_width)
    copied = jnp.broadcast_to(
        pairs_local[:, :, :, None], (2, sequences, kv_heads, sharers, local_rows, head_width)
    )
    heard_pairs = lax.all_to_all(
        copied.reshape(2, cp_devices, local_rows, head_width),
        "cp",
        split_axis=1,
        concat_axis=2,
        tiled=True,
    )
    full_pairs = heard_pairs.reshape(2, length, head_width)
    positions = jnp.arange(block_count, dtype=jnp.int32)
    inverse = jnp.zeros((block_count,), jnp.int32).at[old_block].set(positions)
    query_seq = rotate(regroup(heard_queries, inverse))
    key_seq = rotate(regroup(full_pairs[0], inverse))
    value_seq = regroup(full_pairs[1], inverse)
    attended = causal_attend(query_seq, key_seq, value_seq)
    relaid = regroup(attended, new_block)
    returned_here = lax.all_to_all(relaid, "cp", split_axis=1, concat_axis=0, tiled=True)
    returned = from_behind(returned_here, "pp", 1)
    return returned.reshape(1, sequences, query_heads, local_rows, head_width)


def solution(mesh):
    return jax.shard_map(
        per_device,
        mesh=mesh,
        in_specs=(P("pp", None, None, "cp", None), P("pp", None, None, None, "cp", None), P(), P()),
        out_specs=P("pp", None, None, "cp", None),
        check_vma=False,
    )
```

profile of v0, /device:TPU:1, one launch (start us, length us, event | category | flops | bytes accessed | tf_op | source)
XLA Modules:
  0.0 305.9 jit_solution(16460065307012909908)
XLA Ops:
  0.0 17.8 %all-to-all-start = ((bf16[64,64,128]{2,1,0:T(8,128)(2,1)}), bf16[64,64,128]{2,1,0:T(8,128)(2,1)S(1)}, u32[]{:S(2)}, u32[]{:S(2)}) async-start(bf16[64,64,128]{2,1,0:T(8,128)(2,1)} %bitcast.77), calls=%async_computation | async-start | bytes 2097152 | tf_op jit(solution)/shard_map/all_to_all | solution.py:104
  17.8 31.3 %all-to-all-done = bf16[64,64,128]{2,1,0:T(8,128)(2,1)S(1)} async-done(((bf16[64,64,128]{2,1,0:T(8,128)(2,1)}), bf16[64,64,128]{2,1,0:T(8,128)(2,1)S(1)}, u32[]{:S(2)}, u32[]{:S(2)}) %all-to-all-start) | async-done | bytes 1048608 | tf_op jit(solution)/shard_map/all_to_all | solution.py:104
  49.1 1.9 broadcast_in_dim.54
  50.9 8.2 %all-to-all-start.1 = ((bf16[2,64,64,128]{3,2,0,1:T(8,128)(2,1)}), bf16[2,64,64,128]{3,2,0,1:T(8,128)(2,1)S(1)}, u32[]{:S(2)}, u32[]{:S(2)}) async-start(bf16[2,64,64,128]{3,2,0,1:T(8,128)(2,1)} %bitcast.65), calls=%async_computation.1 | async-start | bytes 4194304 | tf_op jit(solution)/shard_map/all_to_all | solution.py:109
  59.2 1.0 scatter_custom_fusion
  60.3 0.6 pad_clamp_fusion
  60.9 0.6 compare_and_fusion
  61.5 2.0 gather_fusion
  63.9 8.8 %subtract_convert_fusion.1 = (bf16[1,4096,64]{2,1,0:T(8,128)(2,1)S(1)}, bf16[1,4096,64]{2,1,0:T(8,128)(2,1)S(1)}) fusion(f32[1,4096,128]{2,1,0:T(8,128)S(1)} %bitcast_convert_fusion.1, f32[64]{0:T(128)S(1)} %multiply_exponential_fusion), kind=kLoop, calls=%fused_computation.33 | loop fusion | flops 2359296 | bytes 3145984 | tf_op jit(solution)/shard_map/convert.4
  72.6 1.5 pad_maximum_fusion
  74.2 52.6 %all-to-all-done.1 = bf16[2,64,64,128]{3,2,0,1:T(8,128)(2,1)S(1)} async-done(((bf16[2,64,64,128]{3,2,0,1:T(8,128)(2,1)}), bf16[2,64,64,128]{3,2,0,1:T(8,128)(2,1)S(1)}, u32[]{:S(2)}, u32[]{:S(2)}) %all-to-all-start.1) | async-done | bytes 2097184 | tf_op jit(solution)/shard_map/all_to_all | solution.py:109
  126.8 1.2 fusion.22
  127.9 0.8 gather_fusion.1
  128.7 0.5 copy-done.1
  129.1 0.8 gather_fusion.2
  130.4 8.6 %subtract_convert_fusion = (bf16[4096,64]{1,0:T(8,128)(2,1)S(1)}, bf16[4096,64]{1,0:T(8,128)(2,1)S(1)}) fusion(f32[4096,128]{1,0:T(8,128)S(1)} %bitcast_convert_fusion, f32[64]{0:T(128)S(1)} %multiply_exponential_fusion), kind=kLoop, calls=%fused_computation.28 | loop fusion | flops 2359296 | bytes 3145984 | tf_op jit(solution)/shard_map/convert.2
  139.0 0.6 pad_maximum_fusion.1
  139.8 45.7 %while.48 = (s32[]{:T(128)}, bf16[1,4096,128]{2,1,0:T(8,128)(2,1)S(1)}, bf16[1,4096,128]{2,1,0:T(8,128)(2,1)}, bf16[4096,128]{1,0:T(8,128)(2,1)S(1)}, bf16[4096,...) while((s32[]{:T(128)}, ...), condition=%wide.region_6.0_spmd.clone.clone, body=%wide.region_1.8_spmd.clone.clone.sunk | while | flops 136579072 | bytes 5032458 | solution.py:88
  139.8 0.9 constant_dynamic-slice_fusion.2
  140.8 1.0 while.49
  142.0 0.9 constant_dynamic-slice_fusion.2
  143.0 2.0 while.49
  144.6 0.4 fusion.34
  145.2 0.9 constant_dynamic-slice_fusion.2
  146.2 3.0 while.49
  148.8 0.4 fusion.34
  149.4 0.9 constant_dynamic-slice_fusion.2
  150.4 4.0 %while.49 = (s32[]{:T(128)}, f32[1,512]{1,0:T(1,128)S(1)}, f32[1,512]{1,0:T(1,128)S(1)}, f32[1,512,128]{2,1,0:T(8,128)S(1)}, s32[]{:T(128)}, /*index=5*/s32[512]...) while((s32[]{:T(128)}, f32[1,512]{1,0:T(1,128)S(1)}, ...), condition=%wide.region_5.7_spmd, body=%wide.region_2.6_spmd.sunk | while | flops 136447488 | bytes 4104383 | solution.py:84
  154.6 0.9 constant_dynamic-slice_fusion.2
  155.6 5.0 %while.49 = (s32[]{:T(128)}, f32[1,512]{1,0:T(1,128)S(1)}, f32[1,512]{1,0:T(1,128)S(1)}, f32[1,512,128]{2,1,0:T(8,128)S(1)}, s32[]{:T(128)}, /*index=5*/s32[512]...) while((s32[]{:T(128)}, f32[1,512]{1,0:T(1,128)S(1)}, ...), condition=%wide.region_5.7_spmd, body=%wide.region_2.6_spmd.sunk | while | flops 136447488 | bytes 4104383 | solution.py:84
  158.2 0.4 fusion.34
  160.8 0.9 constant_dynamic-slice_fusion.2
  161.8 6.0 %while.49 = (s32[]{:T(128)}, f32[1,512]{1,0:T(1,128)S(1)}, f32[1,512]{1,0:T(1,128)S(1)}, f32[1,512,128]{2,1,0:T(8,128)S(1)}, s32[]{:T(128)}, /*index=5*/s32[512]...) while((s32[]{:T(128)}, f32[1,512]{1,0:T(1,128)S(1)}, ...), condition=%wide.region_5.7_spmd, body=%wide.region_2.6_spmd.sunk | while | flops 136447488 | bytes 4104383 | solution.py:84
  165.4 0.4 fusion.34
  168.0 0.9 constant_dynamic-slice_fusion.2
  169.0 7.0 %while.49 = (s32[]{:T(128)}, f32[1,512]{1,0:T(1,128)S(1)}, f32[1,512]{1,0:T(1,128)S(1)}, f32[1,512,128]{2,1,0:T(8,128)S(1)}, s32[]{:T(128)}, /*index=5*/s32[512]...) while((s32[]{:T(128)}, f32[1,512]{1,0:T(1,128)S(1)}, ...), condition=%wide.region_5.7_spmd, body=%wide.region_2.6_spmd.sunk | while | flops 136447488 | bytes 4104383 | solution.py:84
  171.6 0.4 fusion.34
  176.2 0.9 constant_dynamic-slice_fusion.2
  177.2 8.0 %while.49 = (s32[]{:T(128)}, f32[1,512]{1,0:T(1,128)S(1)}, f32[1,512]{1,0:T(1,128)S(1)}, f32[1,512,128]{2,1,0:T(8,128)S(1)}, s32[]{:T(128)}, /*index=5*/s32[512]...) while((s32[]{:T(128)}, f32[1,512]{1,0:T(1,128)S(1)}, ...), condition=%wide.region_5.7_spmd, body=%wide.region_2.6_spmd.sunk | while | flops 136447488 | bytes 4104383 | solution.py:84
  185.4 0.9 gather_fusion.3
  186.6 16.7 %copy.10 = bf16[1,4096,128]{2,0,1:T(2,128)(2,1)S(1)} copy(bf16[1,4096,128]{2,1,0:T(8,128)(2,1)S(1)} %bitcast.69) | data formatting | bytes 2097152 | tf_op jit(solution)/shard_map/reshape | solution.py:21
  203.3 0.5 broadcast.145
  203.8 22.4 %reduce.4 = bf16[4096,128]{1,0:T(8,128)(2,1)S(1)} reduce(bf16[4096,1,128]{2,1,0:T(2,128)(2,1)S(1)} %bitcast.66, bf16[]{:T(256)} %broadcast.145), dimensions={1}, to_apply=%bitcast.46.reduce_sub_computation | reduce | bytes 2097154
  226.5 48.5 %all_to_all.30 = bf16[64,2,4096]{2,1,0:T(2,128)(2,1)S(1)} all-to-all(bf16[64,2,4096]{2,1,0:T(2,128)(2,1)S(1)} %reshape.272), channel_id=1, replica_groups=mesh['pp'=8,'cp'=64] {'cp'}, dimensions={0} | all-to-all | bytes 2097152 | tf_op jit(solution)/shard_map/all_to_all | solution.py:124
  275.0 1.0 reshape.273
  276.2 1.9 collective-permute-start
  278.2 26.8 %collective-permute-done = bf16[64,64,128]{2,1,0:T(8,128)(2,1)S(1)} collective-permute-done((bf16[64,64,128]{2,1,0:T(8,128)(2,1)S(1)}, bf16[64,64,128]{2,1,0:T(8,128)(2,1)S(1)}, u32[]{:S(2)}, u32[]{:S(2)}) %collective-permute-start) | collective-permute-done | bytes 1048608 | tf_op jit(solution)/shard_map/ppermute | solution.py:11
  305.0 1.0 copy.33
  (322 shorter events, 35.4 us)
Async XLA Ops:
  0.0 17.8 %copy-start.2 = (bf16[1,2,2,4,64,128]{5,4,3,2,1,0:T(8,128)(2,1)S(1)}, bf16[1,2,2,4,64,128]{5,4,3,2,1,0:T(8,128)(2,1)}, u32[]{:S(2)}) copy-start(bf16[1,2,2,4,64,128]{5,4,3,2,1,0:T(8,128)(2,1)} %param.13) | copy-start | bytes 786436
  0.0 49.1 %all-to-all-start = ((bf16[64,64,128]{2,1,0:T(8,128)(2,1)}), bf16[64,64,128]{2,1,0:T(8,128)(2,1)S(1)}, u32[]{:S(2)}, u32[]{:S(2)}) async-start(bf16[64,64,128]{2,1,0:T(8,128)(2,1)} %bitcast.77), calls=%async_computation | async-start | bytes 2097152 | tf_op jit(solution)/shard_map/all_to_all | solution.py:104
  49.1 1.9 copy-start
  50.9 8.3 %copy-start.4 = (s32[128]{0:T(128)S(1)}, s32[128]{0:T(128)}, u32[]{:S(2)}) copy-start(s32[128]{0:T(128)} %param.14) | copy-start | bytes 1540
  50.9 9.3 %copy-start.5 = (s32[128]{0:T(128)S(1)}, s32[128]{0:T(128)}, u32[]{:S(2)}) copy-start(s32[128]{0:T(128)} %param.15) | copy-start | bytes 1540
  50.9 75.8 %all-to-all-start.1 = ((bf16[2,64,64,128]{3,2,0,1:T(8,128)(2,1)}), bf16[2,64,64,128]{3,2,0,1:T(8,128)(2,1)S(1)}, u32[]{:S(2)}, u32[]{:S(2)}) async-start(bf16[2,64,64,128]{3,2,0,1:T(8,128)(2,1)} %bitcast.65), calls=%async_computation.1 | async-start | bytes 4194304 | tf_op jit(solution)/shard_map/all_to_all | solution.py:109
  127.9 1.2 copy-start.1
  185.4 0.9 copy-start.3
  276.2 28.7 %collective-permute-start = (bf16[64,64,128]{2,1,0:T(8,128)(2,1)S(1)}, bf16[64,64,128]{2,1,0:T(8,128)(2,1)S(1)}, u32[]{:S(2)}, u32[]{:S(2)}) collective-permute-start(bf16[64,64,128]{2,1,0:T(8,128)(2,1)S(1)} %bitcast.76), channel_id=1, source_target_pairs={{0,64},{64,128},{128,192},{192,256},{256,320},{320,384},{384,448},... | collective-permute-start | bytes 3145736 | tf_op jit(solution)/shard_map/ppermute | solution.py:11
where the time goes:
time: 307 us; the launch traced here: 306 us
  waiting for transfers between devices  111 us (36%)
  other arithmetic  53.7 us (17%)
  blocking collectives  48.5 us (16%)
  local copies, waits for them, and re-layouts  36.4 us (12%)
  starting transfers between devices  27.9 us (9%)
  matrix products  25.8 us (8%)
    all_to_all x1, waiting for transfers between devices, per_device(): lax.all_to_all(copied.reshape(2, cp_devices, local_rows, head_width), 'cp...  52.6 us
    all_to_all x1, blocking collectives, per_device(): lax.all_to_all(relaid, 'cp', split_axis=1, concat_axis=0, tiled=True)  48.5 us
    all_to_all x1, waiting for transfers between devices, per_device(): lax.all_to_all(sent_queries, 'cp', split_axis=0, concat_axis=1, tiled=True)  31.3 us
    ppermute x1, waiting for transfers between devices, from_behind(): return lax.ppermute(value, axis, pairs)  26.8 us
    unnamed x1, other arithmetic  22.4 us
    all_to_all x1, starting transfers between devices, per_device(): lax.all_to_all(sent_queries, 'cp', split_axis=0, concat_axis=1, tiled=True)  17.8 us
    another operation x2, other arithmetic  17.3 us
    reshape x1, local copies, waits for them, and re-layouts, regroup(): return picked.reshape(dims_shape)  16.7 us
  transfers between devices with their start and end apart: 3, of which 3 were waited for; matrix products, arithmetic and copies ran while one was open for 5% of the time, Pallas kernels for 0%

commit v1 on v0

--- a/solution.py
+++ b/solution.py
@@ -121,7 +121,10 @@
     value_seq = regroup(full_pairs[1], inverse)
     attended = causal_attend(query_seq, key_seq, value_seq)
     relaid = regroup(attended, new_block)
-    returned_here = lax.all_to_all(relaid, "cp", split_axis=1, concat_axis=0, tiled=True)
+    returned_here = jnp.concatenate(
+        lax.all_to_all(jnp.stack(jnp.split(relaid, lax.axis_size("cp"), axis=1)), "cp", 0, 0),
+        axis=0,
+    )
     returned = from_behind(returned_here, "pp", 1)
     return returned.reshape(1, sequences, query_heads, local_rows, head_width)
 

time: 307 us -> 267 us (0.87)
  other arithmetic: 53.7 us -> 32.3 us
  local copies, waits for them, and re-layouts: 36.4 us -> 18.7 us
    unnamed x1 -> x0, other arithmetic: 22.4 us -> none
    reshape x1 -> x0, local copies, waits for them, and re-layouts: 16.7 us -> none  [regroup(): return picked.reshape(dims_shape)]
  transfers between devices with their start and end apart: 3 -> 3, of which waited for: 3 -> 3; matrix products, arithmetic and copies ran while one was open for 5% -> 6% of each run, Pallas kernels for 0% -> 0%
where the time goes in v1:
time: 267 us; the launch traced here: 266 us
  waiting for transfers between devices  110 us (41%)
  blocking collectives  48.7 us (18%)
  other arithmetic  32.3 us (12%)
  starting transfers between devices  27.9 us (10%)
  matrix products  25.8 us (10%)
  local copies, waits for them, and re-layouts  18.7 us (7%)
  loops' own time  2.67 us (1%)
    all_to_all x1, waiting for transfers between devices, per_device(): lax.all_to_all(copied.reshape(2, cp_devices, local_rows, head_width), 'cp...  51.8 us
    all_to_all x1, blocking collectives, per_device(): lax.all_to_all(jnp.stack(jnp.split(relaid, lax.axis_size('cp'), axis=1)),...  48.7 us
    all_to_all x1, waiting for transfers between devices, per_device(): lax.all_to_all(sent_queries, 'cp', split_axis=0, concat_axis=1, tiled=True)  31.3 us
    ppermute x1, waiting for transfers between devices, from_behind(): return lax.ppermute(value, axis, pairs)  26.8 us
    all_to_all x1, starting transfers between devices, per_device(): lax.all_to_all(sent_queries, 'cp', split_axis=0, concat_axis=1, tiled=True)  17.8 us
    another operation x2, other arithmetic  17.2 us
    dot_general x36, matrix products, key_step(): jnp.einsum('hqk,kd->hqd', weights.astype(jnp.bfloat16), value_part, prefe...  14.2 us
    dot_general x36, matrix products, key_step(): jnp.einsum('hqd,kd->hqk', query_part, key_part, preferred_element_type=jn...  11.6 us
  transfers between devices with their start and end apart: 3, of which 3 were waited for; matrix products, arithmetic and copies ran while one was open for 6% of the time, Pallas kernels for 0%

profile of v1, /device:TPU:1, one launch (start us, length us, event | category | flops | bytes accessed | tf_op | source)
XLA Modules:
  0.0 266.5 jit_solution(16452215905135708340)
XLA Ops:
  0.0 17.8 %all-to-all-start = ((bf16[64,64,128]{2,1,0:T(8,128)(2,1)}), bf16[64,64,128]{2,1,0:T(8,128)(2,1)S(1)}, u32[]{:S(2)}, u32[]{:S(2)}) async-start(bf16[64,64,128]{2,1,0:T(8,128)(2,1)} %bitcast.389), calls=%async_computation | async-start | bytes 2097152 | tf_op jit(solution)/shard_map/all_to_all | solution.py:104
  17.8 31.3 %all-to-all-done = bf16[64,64,128]{2,1,0:T(8,128)(2,1)S(1)} async-done(((bf16[64,64,128]{2,1,0:T(8,128)(2,1)}), bf16[64,64,128]{2,1,0:T(8,128)(2,1)S(1)}, u32[]{:S(2)}, u32[]{:S(2)}) %all-to-all-start) | async-done | bytes 1048608 | tf_op jit(solution)/shard_map/all_to_all | solution.py:104
  49.1 1.9 broadcast_in_dim.54
  50.9 8.2 %all-to-all-start.1 = ((bf16[2,64,64,128]{3,2,0,1:T(8,128)(2,1)}), bf16[2,64,64,128]{3,2,0,1:T(8,128)(2,1)S(1)}, u32[]{:S(2)}, u32[]{:S(2)}) async-start(bf16[2,64,64,128]{3,2,0,1:T(8,128)(2,1)} %bitcast.316), calls=%async_computation.1 | async-start | bytes 4194304 | tf_op jit(solution)/shard_map/all_to_all | solution.py:109
  59.2 1.0 scatter_custom_fusion
  60.3 0.6 pad_clamp_fusion
  60.9 0.6 compare_and_fusion
  61.5 1.7 gather_fusion
  63.1 1.4 bitcast_select_fusion.1
  64.8 8.6 %subtract_convert_fusion.1 = (bf16[1,4096,64]{2,1,0:T(8,128)(2,1)S(1)}, bf16[1,4096,64]{2,1,0:T(8,128)(2,1)S(1)}) fusion(f32[1,4096,128]{2,1,0:T(8,128)S(1)} %bitcast_convert_fusion.1, f32[64]{0:T(128)S(1)} %multiply_exponential_fusion), kind=kLoop, calls=%fused_computation.33 | loop fusion | flops 2359296 | bytes 3145984 | tf_op jit(solution)/shard_map/convert.4
  73.3 1.6 pad_maximum_fusion
  74.9 51.8 %all-to-all-done.1 = bf16[2,64,64,128]{3,2,0,1:T(8,128)(2,1)S(1)} async-done(((bf16[2,64,64,128]{3,2,0,1:T(8,128)(2,1)}), bf16[2,64,64,128]{3,2,0,1:T(8,128)(2,1)S(1)}, u32[]{:S(2)}, u32[]{:S(2)}) %all-to-all-start.1) | async-done | bytes 2097184 | tf_op jit(solution)/shard_map/all_to_all | solution.py:109
  126.7 1.2 fusion.22
  127.9 2.0 gather_fusion.1
  129.9 0.8 gather_fusion.2
  131.2 8.6 %subtract_convert_fusion = (bf16[4096,64]{1,0:T(8,128)(2,1)S(1)}, bf16[4096,64]{1,0:T(8,128)(2,1)S(1)}) fusion(f32[4096,128]{1,0:T(8,128)S(1)} %bitcast_convert_fusion, f32[64]{0:T(128)S(1)} %multiply_exponential_fusion), kind=kLoop, calls=%fused_computation.28 | loop fusion | flops 2359296 | bytes 3145984 | tf_op jit(solution)/shard_map/convert.2
  139.7 0.6 pad_maximum_fusion.1
  140.5 45.6 %while.48 = (s32[]{:T(128)}, bf16[1,4096,128]{2,1,0:T(8,128)(2,1)S(1)}, bf16[1,4096,128]{2,1,0:T(8,128)(2,1)}, bf16[4096,128]{1,0:T(8,128)(2,1)S(1)}, bf16[4096,...) while((s32[]{:T(128)}, ...), condition=%wide.region_6.0_spmd.clone.clone, body=%wide.region_1.8_spmd.clone.clone.sunk | while | flops 136579072 | bytes 5032458 | solution.py:88
  140.5 0.9 constant_dynamic-slice_fusion.2
  141.5 1.0 while.49
  142.7 0.9 constant_dynamic-slice_fusion.2
  143.7 2.0 while.49
  145.9 0.9 constant_dynamic-slice_fusion.2
  146.9 3.0 %while.49 = (s32[]{:T(128)}, f32[1,512]{1,0:T(1,128)S(1)}, f32[1,512]{1,0:T(1,128)S(1)}, f32[1,512,128]{2,1,0:T(8,128)S(1)}, s32[]{:T(128)}, /*index=5*/s32[512]...) while((s32[]{:T(128)}, f32[1,512]{1,0:T(1,128)S(1)}, ...), condition=%wide.region_5.7_spmd, body=%wide.region_2.6_spmd.sunk | while | flops 136447488 | bytes 4104383 | solution.py:84
  150.1 0.9 constant_dynamic-slice_fusion.2
  151.1 4.0 %while.49 = (s32[]{:T(128)}, f32[1,512]{1,0:T(1,128)S(1)}, f32[1,512]{1,0:T(1,128)S(1)}, f32[1,512,128]{2,1,0:T(8,128)S(1)}, s32[]{:T(128)}, /*index=5*/s32[512]...) while((s32[]{:T(128)}, f32[1,512]{1,0:T(1,128)S(1)}, ...), condition=%wide.region_5.7_spmd, body=%wide.region_2.6_spmd.sunk | while | flops 136447488 | bytes 4104383 | solution.py:84
  155.3 0.9 constant_dynamic-slice_fusion.2
  156.3 5.0 %while.49 = (s32[]{:T(128)}, f32[1,512]{1,0:T(1,128)S(1)}, f32[1,512]{1,0:T(1,128)S(1)}, f32[1,512,128]{2,1,0:T(8,128)S(1)}, s32[]{:T(128)}, /*index=5*/s32[512]...) while((s32[]{:T(128)}, f32[1,512]{1,0:T(1,128)S(1)}, ...), condition=%wide.region_5.7_spmd, body=%wide.region_2.6_spmd.sunk | while | flops 136447488 | bytes 4104383 | solution.py:84
  160.9 0.4 fusion.34
  161.5 0.9 constant_dynamic-slice_fusion.2
  162.5 6.0 %while.49 = (s32[]{:T(128)}, f32[1,512]{1,0:T(1,128)S(1)}, f32[1,512]{1,0:T(1,128)S(1)}, f32[1,512,128]{2,1,0:T(8,128)S(1)}, s32[]{:T(128)}, /*index=5*/s32[512]...) while((s32[]{:T(128)}, f32[1,512]{1,0:T(1,128)S(1)}, ...), condition=%wide.region_5.7_spmd, body=%wide.region_2.6_spmd.sunk | while | flops 136447488 | bytes 4104383 | solution.py:84
  167.1 0.4 fusion.34
  168.1 0.4 fusion.34
  168.7 0.9 constant_dynamic-slice_fusion.2
  169.7 7.0 %while.49 = (s32[]{:T(128)}, f32[1,512]{1,0:T(1,128)S(1)}, f32[1,512]{1,0:T(1,128)S(1)}, f32[1,512,128]{2,1,0:T(8,128)S(1)}, s32[]{:T(128)}, /*index=5*/s32[512]...) while((s32[]{:T(128)}, f32[1,512]{1,0:T(1,128)S(1)}, ...), condition=%wide.region_5.7_spmd, body=%wide.region_2.6_spmd.sunk | while | flops 136447488 | bytes 4104383 | solution.py:84
  174.3 0.4 fusion.34
  175.3 0.4 fusion.34
  176.3 0.4 fusion.34
  176.9 0.9 constant_dynamic-slice_fusion.2
  177.9 8.0 %while.49 = (s32[]{:T(128)}, f32[1,512]{1,0:T(1,128)S(1)}, f32[1,512]{1,0:T(1,128)S(1)}, f32[1,512,128]{2,1,0:T(8,128)S(1)}, s32[]{:T(128)}, /*index=5*/s32[512]...) while((s32[]{:T(128)}, f32[1,512]{1,0:T(1,128)S(1)}, ...), condition=%wide.region_5.7_spmd, body=%wide.region_2.6_spmd.sunk | while | flops 136447488 | bytes 4104383 | solution.py:84
  182.5 0.4 fusion.34
  184.5 0.4 fusion.34
  185.5 0.4 fusion.34
  186.1 0.9 gather_fusion.3
  188.0 48.7 %all_to_all.23 = bf16[64,1,64,128]{3,2,1,0:T(8,128)(2,1)S(1)} all-to-all(bf16[64,1,64,128]{3,2,1,0:T(8,128)(2,1)S(1)} %constant_dynamic-update-slice_fusion), channel_id=1, replica_groups=mesh['pp'=8,'cp'=64] {'cp'}, dimensions={0} | all-to-all | bytes 2097152 | tf_op jit(solution)/shard_map/all_to_all | solution.py:125
  236.8 1.9 collective-permute-start
  238.7 26.8 %collective-permute-done = bf16[64,64,128]{2,1,0:T(8,128)(2,1)S(1)} collective-permute-done((bf16[64,64,128]{2,1,0:T(8,128)(2,1)S(1)}, bf16[64,64,128]{2,1,0:T(8,128)(2,1)S(1)}, u32[]{:S(2)}, u32[]{:S(2)}) %collective-permute-start) | collective-permute-done | bytes 1048608 | tf_op jit(solution)/shard_map/ppermute | solution.py:11
  265.5 1.0 copy.154
  (376 shorter events, 33.7 us)
Async XLA Ops:
  0.0 17.8 %copy-start = (bf16[1,2,2,4,64,128]{5,4,3,2,1,0:T(8,128)(2,1)S(1)}, bf16[1,2,2,4,64,128]{5,4,3,2,1,0:T(8,128)(2,1)}, u32[]{:S(2)}) copy-start(bf16[1,2,2,4,64,128]{5,4,3,2,1,0:T(8,128)(2,1)} %param.13) | copy-start | bytes 786436
  0.0 49.1 %all-to-all-start = ((bf16[64,64,128]{2,1,0:T(8,128)(2,1)}), bf16[64,64,128]{2,1,0:T(8,128)(2,1)S(1)}, u32[]{:S(2)}, u32[]{:S(2)}) async-start(bf16[64,64,128]{2,1,0:T(8,128)(2,1)} %bitcast.389), calls=%async_computation | async-start | bytes 2097152 | tf_op jit(solution)/shard_map/all_to_all | solution.py:104
  50.9 8.3 %copy-start.2 = (s32[128]{0:T(128)S(1)}, s32[128]{0:T(128)}, u32[]{:S(2)}) copy-start(s32[128]{0:T(128)} %param.14) | copy-start | bytes 1540
  50.9 9.3 %copy-start.3 = (s32[128]{0:T(128)S(1)}, s32[128]{0:T(128)}, u32[]{:S(2)}) copy-start(s32[128]{0:T(128)} %param.15) | copy-start | bytes 1540
  50.9 75.8 %all-to-all-start.1 = ((bf16[2,64,64,128]{3,2,0,1:T(8,128)(2,1)}), bf16[2,64,64,128]{3,2,0,1:T(8,128)(2,1)S(1)}, u32[]{:S(2)}, u32[]{:S(2)}) async-start(bf16[2,64,64,128]{3,2,0,1:T(8,128)(2,1)} %bitcast.316), calls=%async_computation.1 | async-start | bytes 4194304 | tf_op jit(solution)/shard_map/all_to_all | solution.py:109
  186.1 0.9 copy-start.1
  236.8 28.7 %collective-permute-start = (bf16[64,64,128]{2,1,0:T(8,128)(2,1)S(1)}, bf16[64,64,128]{2,1,0:T(8,128)(2,1)S(1)}, u32[]{:S(2)}, u32[]{:S(2)}) collective-permute-start(bf16[64,64,128]{2,1,0:T(8,128)(2,1)S(1)} %bitcast.390), channel_id=1, source_target_pairs={{0,64},{64,128},{128,192},{192,256},{256,320},{320,384},{384,448},... | collective-permute-start | bytes 3145736 | tf_op jit(solution)/shard_map/ppermute | solution.py:11
